TPU v7x, 256 devices: a whole 4x4x8 slice. The times are simulated.
256 devices in a mesh: section: 8 (over x, core), tp: 4 (over z_lo), fsdp: 8 (over y, z_hi).
Axes of the slice: x: 4, y: 4, z: 8 (z_hi: 2, z_lo: 4; z = z_hi * 4 + z_lo), core: 2. Of those that a mesh axis runs over, the one named last changes fastest.
Arguments:
- teacher_updates: bfloat16 [8, 256, 4, 16384], P('section', 'fsdp', None, 'tp'), may hold values from -6 to 6
- layer_map: int32 [8, 32], replicated, may hold values from 0 to 7
- route: int32 [8, 32], replicated, may hold values from 0 to 7, as said below
- projector: bfloat16 [16384, 5120], P('tp', 'section'), may hold values from -0.046875 to 0.046875
- student_in: bfloat16 [8, 8, 16, 5120], P('fsdp'), may hold values from -6 to 6
- norm_gain: float32 [5120], replicated, may hold values from 0.25 to 1.75
- w_gate: bfloat16 [5120, 12800], P('fsdp', ('section', 'tp')), may hold values from -0.078125 to 0.078125
- w_up: bfloat16 [5120, 12800], P('fsdp', ('section', 'tp')), may hold values from -0.078125 to 0.078125
- w_down: bfloat16 [12800, 5120], P(('section', 'tp'), 'fsdp'), may hold values from -0.0546875 to 0.0546875
Outputs:
- gate_grad: float32 [5120, 12800], P('fsdp', ('section', 'tp'))
- up_grad: float32 [5120, 12800], P('fsdp', ('section', 'tp'))
- down_grad: float32 [12800, 5120], P(('section', 'tp'), 'fsdp')
Inputs may be any that keep to these rules, and one draw needn't show every extreme that they name: Each row of route names every student shard exactly 4 times: every teacher column sends 4 micro-batches to each student shard.
All inputs are finite; a program needn't handle non-finite values.
Results may differ from a plain program's by a relative error of at most 0.023.
Values may be sent and summed in bfloat16 or wider, within the bound.
A program may use at most 128 MiB of HBM per device.

v0:
```python
import jax
import jax.numpy as jnp
from jax import lax
from jax.experimental import pallas as pl
from jax.experimental.pallas import tpu as pltpu
from jax.sharding import PartitionSpec as P

MESH = pl.DeviceIdType.MESH
EPS = 1e-05
F32 = jnp.float32
BF16 = jnp.bfloat16

TW = 4096
SW = 640
SUB = 80
HW = 400
TEACHER_WIDTH = 16384
STUDENT_WIDTH = 5120
ROWS = 4

NN = (((1,), (0,)), ((), ()))
NT = (((1,), (1,)), ((), ()))
TN = (((0,), (0,)), ((), ()))


def dot(a, b, dims):
    return lax.dot_general(a, b, dims, preferred_element_type=F32)


SCRATCH = (
    ("updv", (32, 4, TW), BF16),
    ("projv", (TW, SW), BF16),
    ("wg", (HW, SW), BF16),
    ("wu", (HW, SW), BF16),
    ("wd", (HW, SW), BF16),
    ("u", (8, 16, TW), BF16),
    ("t1r", (8, 16, TW), BF16),
    ("pk", (8, 16, TW), BF16),
    ("prs", (4, 32, SW + 256), BF16),
    ("t3r", (3, 32, SW + 256), BF16),
    ("t4s", (32, SW), BF16),
    ("t4r", (32, SW), BF16),
    ("xr", (2, 16, SW), BF16),
    ("a1s", (7, SUB, 128), BF16),
    ("nt", (4, 2, 8, SUB, 128), BF16),
    ("g1", (2, 4, 2 * HW, 128), BF16),
    ("gr", (2, 3, 2 * HW, 128), BF16),
    ("gzs", (2 * HW, 128), BF16),
    ("gzr", (2 * HW, 128), BF16),
    ("aa", (4, 2, 2 * HW, 128), BF16),
    ("ht", (4, 2, HW, 128), BF16),
    ("pb0", (8, 4, 2, 16, 384), BF16),
    ("d1r0", (8, 4, 16, 384), BF16),
    ("q0", (8, 4, 16, 384), BF16),
    ("d2r0", (3, 8, 16, 384), BF16),
    ("r0", (4, 2, 16, 384), BF16),
    ("d3r0", (3, 2, 16, 384), BF16),
    ("dl0", (8, 8, 16, 384), BF16),
    ("pb1", (8, 4, 2, 16, 256), BF16),
    ("d1r1", (8, 4, 16, 256), BF16),
    ("q1", (8, 4, 16, 256), BF16),
    ("d2r1", (3, 8, 16, 256), BF16),
    ("r1", (4, 2, 16, 256), BF16),
    ("d3r1", (3, 2, 16, 256), BF16),
    ("dl1", (8, 8, 16, 256), BF16),
    ("hacc", (2, HW, 512), F32),
    ("down", (HW, SW), F32),
    ("h1", (2, 4, HW, 128), BF16),
    ("hr", (2, 3, HW, 128), BF16),
    ("hzs", (HW, 128), BF16),
    ("hzr", (HW, 128), BF16),
    ("dh", (4, 2, HW, 128), BF16),
)
N_SEM = 192
OUTS = (
    ((4, 2, 8, SUB, 128), BF16),
    ((HW, SW), F32),
    ((4, 2, 2 * HW, 128), BF16),
    ((4, 2, HW, 128), BF16),
)
HALF = 208
HIDDEN = ((0, HALF), (HALF, HW))
BOTH = ((0, 2 * HALF), (2 * HALF, 2 * HW))
COLUMNS = ((0, 384), (384, SW))


class Refs:
    pass


def selection(layer_map, route, f, s):
    lane = lax.broadcasted_iota(jnp.int32, (32, 128), 1)
    slot = lax.broadcasted_iota(jnp.int32, (32, 128), 0)
    widen = jnp.where(lane // ROWS == slot, 1.0, 0.0).astype(BF16)
    mine = lax.broadcasted_iota(jnp.int32, (8, 128), 0) == f

    def row(table):
        wide = dot(table[...].astype(F32).astype(BF16), widen, NN)
        return jnp.sum(jnp.where(mine, wide, 0.0), axis=0, keepdims=True)

    dest, layer = row(route), row(layer_map)
    across = jnp.broadcast_to(dest, (128, 128))
    a = lax.broadcasted_iota(jnp.int32, (128, 128), 0)
    c = lax.broadcasted_iota(jnp.int32, (128, 128), 1)
    earlier = (across.T == across) & (a // ROWS < c // ROWS) & (a % ROWS == 0)
    rank = jnp.sum(jnp.where(earlier, 1.0, 0.0), axis=0, keepdims=True)
    place = (dest * 4.0 + rank) * ROWS + (c[0:1] % ROWS).astype(F32)
    place = jnp.where(layer >= s.astype(F32), place, -1.0)
    return jnp.where(a.astype(F32) == place, 1.0, 0.0).astype(BF16)


def kernel(upd, layer_map, route, proj, xin, gain, wg, wu, wd, *rest):
    outs, scratch = rest[: len(OUTS)], rest[len(OUTS) :]
    b = Refs()
    for (name, _, _), ref in zip(SCRATCH, scratch):
        setattr(b, name, ref)
    send_sem, recv_sem, in_sem, out_sem = scratch[len(SCRATCH) :]
    s = lax.axis_index("section")
    t = lax.axis_index("tp")
    f = lax.axis_index("fsdp")
    x, core = s // 2, s % 2
    y, zh = f // 2, f % 2
    far_z = 1 - zh
    used = [2]
    started = []

    def describe(src, dst, dev, sem=None):
        if sem is None:
            sem = used[0]
            used[0] += 1
        return pltpu.make_async_remote_copy(
            src_ref=src,
            dst_ref=dst,
            send_sem=send_sem.at[sem],
            recv_sem=recv_sem.at[sem],
            device_id=dev,
            device_id_type=MESH,
        )

    def send(src, dst, dev):
        copy = describe(src, dst, dev)
        copy.start()
        started.append(copy)
        return copy

    def on_x(o):
        return {"section": (x + o) % 4 * 2 + core}

    def on_y(o):
        return {"fsdp": (y + o) % 4 * 2 + zh}

    def on_tp(o):
        return {"tp": (t + o) % 4}

    other_core = {"section": x * 2 + 1 - core}
    other_z = {"fsdp": y * 2 + far_z}
    swapped = {"section": f, "fsdp": s}

    barrier = pltpu.get_barrier_semaphore()
    for o in range(1, 8):
        pl.semaphore_signal(barrier, inc=1, device_id={"section": (s + o) % 8}, device_id_type=MESH)
        pl.semaphore_signal(barrier, inc=1, device_id={"fsdp": (f + o) % 8}, device_id_type=MESH)
    for o in range(1, 4):
        pl.semaphore_signal(barrier, inc=1, device_id=on_tp(o), device_id_type=MESH)

    @pl.when(s != f)
    def _():
        pl.semaphore_signal(barrier, inc=1, device_id=swapped, device_id_type=MESH)

    loads = {}
    for k, (name, src, dst) in enumerate(
        (("wg", wg, b.wg), ("wu", wu, b.wu), ("upd", upd, b.updv), ("proj", proj, b.projv), ("wd", wd, b.wd))
    ):
        loads[name] = pltpu.make_async_copy(src, dst, in_sem.at[k])
        loads[name].start()

    def student(k):
        return xin[:, :, k * SW : (k + 1) * SW].reshape(128, SW).astype(F32)

    total = jnp.zeros((128, 128), F32)
    for k in range(8):
        v = student(k)
        for c in range(0, SW, 128):
            total = total + v[:, c : c + 128] * v[:, c : c + 128]
    total = jnp.sum(total, axis=1, keepdims=True)
    inv = lax.rsqrt(total / STUDENT_WIDTH + EPS)
    rows = lax.broadcasted_iota(jnp.int32, (SUB, SW), 0)
    cols = lax.broadcasted_iota(jnp.int32, (SUB, SW), 1)
    sel = jnp.where(cols == rows + s * SUB, 1.0, 0.0).astype(BF16)
    pl.semaphore_wait(barrier, jnp.where(s == f, 17, 18))

    a1 = {}
    order = ((1, 0), (1, 1), (1, 3), (1, 2), (0, 1), (0, 3), (0, 2), (0, 0))
    for n, (dz, dy) in enumerate(order):
        k = (y + dy) % 4 * 2 + (zh + dz) % 2
        lanes = pl.ds(pl.multiple_of(k * SW, 128), SW)
        v = xin[:, :, lanes].reshape(128, SW).astype(F32)
        piece = dot(sel, (v * inv * gain[:, lanes]).astype(BF16), NT).astype(BF16)
        if n < 7:
            b.a1s[n] = piece
            a1[dz, dy] = send(b.a1s.at[n], b.nt.at[y, zh, s], {"fsdp": k})
        else:
            b.nt[y, zh, s] = piece

    xsends = []
    for o in range(1, 8):
        k = (f + o) % 8
        c = pltpu.make_async_remote_copy(
            src_ref=xin.at[s, :, pl.ds(pl.multiple_of(k * SW, 128), SW)],
            dst_ref=b.xr.at[zh],
            send_sem=send_sem.at[used[0]],
            recv_sem=recv_sem.at[zh],
            device_id={"fsdp": k},
            device_id_type=MESH,
        )
        used[0] += 1
        xsends.append(c)

    @pl.when(y == t)
    def _():
        for c in xsends:
            c.start()
        b.xr[zh] = xin[s, :, pl.ds(pl.multiple_of(f * SW, 128), SW)]

    def spread_start(at):
        copies = [send(at(s), at(s), on_x(o)) for o in range(1, 4)]
        across = [send(at(s), at(s), other_core)]
        return at, copies, across

    def spread_forward(state):
        at, copies, across = state
        for o in range(1, 4):
            copies[o - 1].wait_recv()
            k = (x - o + 4) % 4 * 2 + core
            across.append(send(at(k), at(k), other_core))

    def spread_end(state):
        for c in state[2]:
            c.wait_recv()

    for dy in (1, 2, 3):
        a1[0, dy].wait_recv()
    near = spread_start(lambda k: b.nt.at[:, zh, k])

    perm = selection(layer_map, route, f, s)
    loads["upd"].wait()
    for k in range(4):
        cut = slice(k * (TW // 4), (k + 1) * (TW // 4))
        part = b.updv[:, :, cut].reshape(128, TW // 4)
        b.u[:, :, cut] = dot(perm, part, NN).astype(BF16).reshape(8, 16, TW // 4)

    for dy in (0, 1, 2, 3):
        a1[1, dy].wait_recv()
    far = spread_start(lambda k: b.nt.at[:, far_z, k])
    loads["wg"].wait()
    loads["wu"].wait()

    def rows_of(chunk):
        return pl.ds(chunk[0], chunk[1] - chunk[0])

    def reduce_send(src, got, h, chunk):
        part = rows_of(chunk)
        return [send(src.at[h, (y + o) % 4, part], got.at[h, o - 1, part], on_y(o)) for o in (2, 1, 3)]

    def partial_sum(src, got, h, low, high):
        acc = src[h, y, low:high].astype(F32)
        for o in range(3):
            acc = acc + got[h, o, low:high].astype(F32)
        return acc

    def reduce_across(copies, src, got, zs, zr, chunk):
        for c in copies:
            c.wait_recv()
        for k in range(chunk[0], chunk[1], 16 * 13):
            top = min(k + 16 * 13, chunk[1])
            zs[k:top] = partial_sum(src, got, 0, k, top).astype(BF16)
        return send(zs.at[rows_of(chunk)], zr.at[rows_of(chunk)], other_z)

    def gather_start(buf, chunk):
        own = buf.at[y, zh, rows_of(chunk)]
        far = send(own, own, other_z)
        return buf, chunk, far, [send(own, own, on_y(o)) for o in (2, 1, 3)]

    def gather_forward(state):
        buf, chunk, far, copies = state
        far.wait_recv()
        got = buf.at[y, far_z, rows_of(chunk)]
        copies += [send(got, got, on_y(o)) for o in (2, 1, 3)]

    def gather_end(state):
        for c in state[3]:
            c.wait_recv()

    def gate_up(h, z):
        four = jnp.concatenate([b.nt[k, z].reshape(SW, 128) for k in range(4)], axis=1)
        for w, put in ((b.wg, 0), (b.wu, 1)):
            r = dot(w[...], four, NN).astype(BF16)
            for k in range(4):
                lanes = slice(128 * k, 128 * (k + 1))
                b.g1[h, k, put * HALF : (put + 1) * HALF] = r[:HALF, lanes]
                low = 2 * HALF + put * (HW - HALF)
                b.g1[h, k, low : low + HW - HALF] = r[HALF:, lanes]

    spread_forward(near)
    spread_end(near)
    gate_up(1, zh)
    spread_forward(far)
    t1 = []
    for o in range(1, 8):
        k = (s + o) % 8
        t1.append(send(b.u.at[k], b.t1r.at[s], {"section": k}))
    spread_end(far)
    gate_up(0, far_z)
    far_rows = [reduce_send(b.g1, b.gr, 0, chunk) for chunk in BOTH]
    near_rows = [reduce_send(b.g1, b.gr, 1, chunk) for chunk in BOTH]
    stores = [pltpu.make_async_copy(b.nt, outs[0], out_sem.at[0])]
    stores[0].start()
    across = [reduce_across(far_rows[0], b.g1, b.gr, b.gzs, b.gzr, BOTH[0])]

    for c in t1:
        c.wait_recv()
    for k in range(4):
        cut = slice(k * (TW // 4), (k + 1) * (TW // 4))
        acc = b.u[s, :, cut].astype(F32)
        for o in range(1, 8):
            acc = acc + b.t1r[(s + o) % 8, :, cut].astype(F32)
        b.pk[s, :, cut] = acc.astype(BF16)
    t2 = spread_start(lambda k: b.pk.at[k])
    across.append(reduce_across(far_rows[1], b.g1, b.gr, b.gzs, b.gzr, BOTH[1]))

    hidden = []
    for n in range(2):
        for c in near_rows[n]:
            c.wait_recv()
        across[n].wait_recv()
        low, mid, high = BOTH[n][0], (BOTH[n][0] + BOTH[n][1]) // 2, BOTH[n][1]
        gate = partial_sum(b.g1, b.gr, 1, low, mid) + b.gzr[low:mid].astype(F32)
        up = partial_sum(b.g1, b.gr, 1, mid, high) + b.gzr[mid:high].astype(F32)
        sig = 1.0 / (1.0 + jnp.exp(-gate))
        b.ht[y, zh, HIDDEN[n][0] : HIDDEN[n][1]] = (gate * sig * up).astype(BF16)
        hidden.append(gather_start(b.ht, HIDDEN[n]))
        b.aa[y, zh, low:mid] = (up * sig * (1.0 + gate * (1.0 - sig))).astype(BF16)
        b.aa[y, zh, mid:high] = (gate * sig).astype(BF16)
    gather_forward(hidden[0])
    spread_forward(t2)
    gather_forward(hidden[1])
    own_factors = b.aa.at[y, zh]
    far_factors = send(own_factors, own_factors, other_z)

    spread_end(t2)
    squares = jnp.zeros((128, 1), F32)
    for k in range(4):
        v = b.pk[:, :, k * (TW // 4) : (k + 1) * (TW // 4)].reshape(128, TW // 4).astype(F32)
        squares = squares + jnp.sum(v * v, axis=1, keepdims=True)
    squares = jnp.broadcast_to(squares, (128, 128))
    high = squares.astype(BF16)
    b.prs[:, :, SW : SW + 128] = high.reshape(4, 32, 128)
    b.prs[:, :, SW + 128 :] = (squares - high.astype(F32)).astype(BF16).reshape(4, 32, 128)
    loads["proj"].wait()
    b.prs[:, :, :SW] = dot(b.pk[...].reshape(128, TW), b.projv[...], NN).astype(BF16).reshape(4, 32, SW)
    t3 = [send(b.prs.at[(t + o) % 4], b.t3r.at[o - 1], on_tp(o)) for o in range(1, 4)]
    loads["wd"].wait()
    for n in range(2):
        gather_end(hidden[n])

    pb, d1r, q = (b.pb0, b.pb1), (b.d1r0, b.d1r1), (b.q0, b.q1)
    d2r, r, d3r, dl = (b.d2r0, b.d2r1), (b.r0, b.r1), (b.d3r0, b.d3r1), (b.dl0, b.dl1)
    factors = (b.aa, (0, 2 * HW), far_factors, [send(own_factors, own_factors, on_y(o)) for o in (2, 1, 3)])
    units = jnp.concatenate([b.ht[k // 2, k % 2] for k in range(8)], axis=1)
    d1 = []
    for n, (low, high) in enumerate(COLUMNS):
        m = dot(units, b.wd[:, low:high], TN).astype(BF16)
        pb[n][...] = m.reshape(8, 4, 2, 16, high - low)
        d1.append(send(pb[n].at[:, :, 1 - core], d1r[n], other_core))
    d2 = []
    for n in range(2):
        d1[n].wait_recv()
        for k in range(8):
            q[n][k] = (pb[n][k, :, core].astype(F32) + d1r[n][k].astype(F32)).astype(BF16)
        d2.append([send(q[n].at[:, (x + o) % 4], d2r[n].at[o - 1], on_x(o)) for o in (2, 1, 3)])

    for c in t3:
        c.wait_recv()
    acc = b.prs[t].astype(F32)
    for o in range(3):
        acc = acc + b.t3r[o].astype(F32)
    squares = acc[:, SW : SW + 1] + acc[:, SW + 128 : SW + 129]
    b.t4s[...] = (acc[:, :SW] * lax.rsqrt(squares / TEACHER_WIDTH + EPS)).astype(BF16)
    t4 = describe(b.t4s, b.t4r, swapped)

    @pl.when(s != f)
    def _():
        t4.start()

    @pl.when(s == f)
    def _():
        b.t4r[...] = b.t4s[...]

    gather_forward(factors)
    d3 = []
    for n in range(2):
        for c in d2[n]:
            c.wait_recv()
        for k in range(8):
            acc = q[n][k, x].astype(F32)
            for o in range(3):
                acc = acc + d2r[n][o, k].astype(F32)
            r[n][k // 2, k % 2] = acc.astype(BF16)
        d3.append([send(r[n].at[(t + o) % 4], d3r[n].at[o - 1], on_tp(o)) for o in range(1, 4)])

    @pl.when(s != f)
    def _():
        t4.wait_recv()

    for e in range(2):

        @pl.when(f != 2 * t + e)
        def _():
            describe(b.xr.at[e], b.xr.at[e], {"fsdp": (f + 1) % 8}, e).wait_recv()

    e1 = []
    for n, (low, high) in enumerate(COLUMNS):
        for c in d3[n]:
            c.wait_recv()
        for e in range(2):
            acc = r[n][t, e].astype(F32)
            for o in range(3):
                acc = acc + d3r[n][o, e].astype(F32)
            error = b.xr[e, :, low:high].astype(F32) + acc - b.t4r[e * 16 : (e + 1) * 16, low:high].astype(F32)
            dl[n][2 * t + e, s] = (error / ROWS).astype(BF16)
        own = dl[n].at[pl.ds(2 * t, 2), s]
        e1.append([send(own, own, on_tp(o)) for o in range(1, 4)])
    e2 = []
    for n in range(2):
        for c in e1[n]:
            c.wait_recv()
        e2.append(spread_start(lambda k, buf=dl[n]: buf.at[:, k]))

    def d_hidden(n, z):
        low, high = COLUMNS[n]
        four = jnp.concatenate([dl[n][2 * k + z].reshape(128, high - low) for k in range(4)], axis=0)
        return dot(b.wd[:, low:high], four, NT)

    spread_forward(e2[0])
    spread_end(e2[0])
    b.hacc[0] = d_hidden(0, far_z)
    b.hacc[1] = d_hidden(0, zh)
    spread_forward(e2[1])
    spread_end(e2[1])
    copies = []
    for h, z in ((0, far_z), (1, zh)):
        m = (b.hacc[h] + d_hidden(1, z)).astype(BF16)
        for k in range(4):
            b.h1[h, k] = m[:, 128 * k : 128 * (k + 1)]
        copies.append([reduce_send(b.h1, b.hr, h, chunk) for chunk in HIDDEN])
    gather_end(factors)
    stores.append(pltpu.make_async_copy(b.aa, outs[2], out_sem.at[2]))
    stores[-1].start()
    across = [reduce_across(copies[0][n], b.h1, b.hr, b.hzs, b.hzr, HIDDEN[n]) for n in range(2)]

    units = jnp.concatenate([b.ht[k // 2, k % 2] for k in range(8)], axis=1)
    for n, (low, high) in enumerate(COLUMNS):
        b.down[:, low:high] = dot(units, dl[n][...].reshape(1024, high - low), NN)
    stores.append(pltpu.make_async_copy(b.down, outs[1], out_sem.at[1]))
    stores[-1].start()
    last = []
    for n, (low, high) in enumerate(HIDDEN):
        for c in copies[1][n]:
            c.wait_recv()
        across[n].wait_recv()
        b.dh[y, zh, low:high] = (partial_sum(b.h1, b.hr, 1, low, high) + b.hzr[low:high].astype(F32)).astype(BF16)
        last.append(gather_start(b.dh, HIDDEN[n]))
    for n in range(2):
        gather_forward(last[n])
    for n in range(2):
        gather_end(last[n])
        part = rows_of(HIDDEN[n])
        stores.append(pltpu.make_async_copy(b.dh.at[:, :, part], outs[3].at[:, :, part], out_sem.at[3 + n]))
        stores[-1].start()

    for c in started:
        c.wait_send()

    @pl.when(s != f)
    def _():
        t4.wait_send()

    @pl.when(y == t)
    def _():
        for c in xsends:
            c.wait_send()

    for c in stores:
        c.wait()
    assert used[0] <= N_SEM


def gradients(nt, down, aa, dh, gate_o, up_o, down_o, nt_v, aa_v, dh_v, grad_v, down_v, sems):
    loads = [
        pltpu.make_async_copy(src, dst, sems.at[k])
        for k, (src, dst) in enumerate(((dh, dh_v), (aa, aa_v), (nt, nt_v), (down, down_v)))
    ]
    for c in loads:
        c.start()
    loads[0].wait()
    loads[1].wait()

    def hidden_grad(put):
        parts = []
        for n in range(2):
            (low, high), (first, last) = HIDDEN[n], BOTH[n]
            rows = slice(first + put * (high - low), first + (put + 1) * (high - low))
            parts.append(
                jnp.concatenate(
                    [(dh_v[k, low:high].astype(F32) * aa_v[k, rows].astype(F32)).astype(BF16) for k in range(8)],
                    axis=1,
                )
            )
        return jnp.concatenate(parts, axis=0)

    d_gate, d_up = hidden_grad(0), hidden_grad(1)
    loads[3].wait()
    down_store = pltpu.make_async_copy(down_v, down_o, sems.at[6])
    down_store.start()
    loads[2].wait()
    normed = jnp.concatenate([nt_v[k] for k in range(8)], axis=1)
    grad_v[0] = dot(d_gate, normed, NT)
    gate_store = pltpu.make_async_copy(grad_v.at[0], gate_o, sems.at[4])
    gate_store.start()
    grad_v[1] = dot(d_up, normed, NT)
    up_store = pltpu.make_async_copy(grad_v.at[1], up_o, sems.at[5])
    up_store.start()
    down_store.wait()
    gate_store.wait()
    up_store.wait()


def on_device(
    teacher_updates, layer_map, route, projector, student_in, norm_gain, w_gate, w_up, w_down
):
    vmem = pl.BlockSpec(memory_space=pltpu.VMEM)
    hbm = pl.BlockSpec(memory_space=pl.ANY)
    nt, down, aa, dh = pl.pallas_call(
        kernel,
        out_shape=[jax.ShapeDtypeStruct(*out) for out in OUTS],
        in_specs=[hbm, vmem, vmem, hbm, vmem, vmem, hbm, hbm, hbm],
        out_specs=[hbm] * len(OUTS),
        scratch_shapes=[pltpu.VMEM(shape, kind) for _, shape, kind in SCRATCH]
        + [pltpu.SemaphoreType.DMA((n,)) for n in (N_SEM, N_SEM, 5, 5)],
        compiler_params=pltpu.CompilerParams(
            collective_id=0, has_side_effects=True, vmem_limit_bytes=56 * 1024 * 1024
        ),
    )(
        teacher_updates.reshape(32, 4, TW),
        layer_map,
        route,
        projector,
        student_in.reshape(8, 16, STUDENT_WIDTH),
        norm_gain.reshape(1, STUDENT_WIDTH),
        w_gate.T,
        w_up.T,
        w_down,
    )

    gate_grad, up_grad, down_grad = pl.pallas_call(
        gradients,
        out_shape=[jax.ShapeDtypeStruct((HW, SW), F32)] * 3,
        in_specs=[hbm] * 4,
        out_specs=[hbm] * 3,
        scratch_shapes=[
            pltpu.VMEM((8, SW, 128), BF16),
            pltpu.VMEM((8, 2 * HW, 128), BF16),
            pltpu.VMEM((8, HW, 128), BF16),
            pltpu.VMEM((2, HW, SW), F32),
            pltpu.VMEM((HW, SW), F32),
            pltpu.SemaphoreType.DMA((7,)),
        ],
        compiler_params=pltpu.CompilerParams(vmem_limit_bytes=56 * 1024 * 1024),
    )(nt.reshape(8, SW, 128), down, aa.reshape(8, 2 * HW, 128), dh.reshape(8, HW, 128))
    return gate_grad.T, up_grad.T, down_grad


def solution(mesh):
    placed = (
        P("section", "fsdp", None, "tp"),
        P(),
        P(),
        P("tp", "section"),
        P("fsdp", None, None, None),
        P(),
        P("fsdp", ("section", "tp")),
        P("fsdp", ("section", "tp")),
        P(("section", "tp"), "fsdp"),
    )
    return jax.shard_map(
        on_device,
        mesh=mesh,
        in_specs=placed,
        out_specs=(
            P("fsdp", ("section", "tp")),
            P("fsdp", ("section", "tp")),
            P(("section", "tp"), "fsdp"),
        ),
        check_vma=False,
    )
```

profile of v0, /device:TPU:1, one launch (start us, length us, event | category | flops | bytes accessed | tf_op | source)
XLA Modules:
  0.0 124.3 jit_solution(15390209186189824478)
XLA Ops:
  0.6 118.8 %shard_map.112 = (bf16[4,2,8,80,128]{4,3,2,1,0:T(8,128)(2,1)}, f32[400,640]{1,0:T(8,128)}, bf16[4,2,800,128]{3,2,1,0:T(8,128)(2,1)}, bf16[4,2,400,128]{3,2,1,0:T(8,128)(2,1)}) custom-call(bf16[32,4,4096]{2,1,0:T(4,128)(2,1)} %bitcast.13, s32[8,32]{1,0:T(8,128)} %layer_map.1, s32[8,32]{1,0:T(8,128)} %route.1, bf16[4096,640]{1,0:T(8,128)(2,1)} %proj.1, ...), custom_call_target="tpu_custom_call" | custom-call | tf_op jit(solution)/shard_map/pallas_call | solution.py:543
  119.4 4.9 %shard_map.113 = (f32[400,640]{1,0:T(8,128)}, f32[400,640]{1,0:T(8,128)}, f32[400,640]{1,0:T(8,128)}) custom-call(bf16[8,640,128]{2,1,0:T(8,128)(2,1)} %bitcast.11, f32[400,640]{1,0:T(8,128)} %get-tuple-element.11.down, bf16[8,800,128]{2,1,0:T(8,128)(2,1)} %bitcast.10, bf16[8,400,128]{2,1,0:T(8,128)(2,1)} %bitcast.14), custom_call_target="tpu_custom_call" | custom-call | tf_op jit(solution)/shard_map/pallas_call | solution.py:565
where the time goes:
time: 124 us
  Pallas kernels  124 us (100%)
    pallas_call x1, Pallas kernels, on_device(): pl.pallas_call(kernel, out_shape=[jax.ShapeDtypeStruct(*out) for out in O...  119 us
    pallas_call x1, Pallas kernels, on_device(): pl.pallas_call(gradients, out_shape=[jax.ShapeDtypeStruct((HW, SW), F32)]...  4.87 us

commit v1 on v0

--- a/solution.py
+++ b/solution.py
@@ -293,13 +293,16 @@
 
     def gate_up(h, z):
         four = jnp.concatenate([b.nt[k, z].reshape(SW, 128) for k in range(4)], axis=1)
-        for w, put in ((b.wg, 0), (b.wu, 1)):
-            r = dot(w[...], four, NN).astype(BF16)
-            for k in range(4):
-                lanes = slice(128 * k, 128 * (k + 1))
-                b.g1[h, k, put * HALF : (put + 1) * HALF] = r[:HALF, lanes]
-                low = 2 * HALF + put * (HW - HALF)
-                b.g1[h, k, low : low + HW - HALF] = r[HALF:, lanes]
+        sent = []
+        for (first, last), (top, end) in zip(HIDDEN, BOTH):
+            for put, w in enumerate((b.wg, b.wu)):
+                m = dot(w[first:last], four, NN).astype(BF16)
+                low = top + put * (last - first)
+                for k in range(4):
+                    b.g1[h, k, low : low + last - first] = m[:, 128 * k : 128 * (k + 1)]
+            if h == 0:
+                sent.append(reduce_send(b.g1, b.gr, h, (top, end)))
+        return sent
 
     spread_forward(near)
     spread_end(near)
@@ -310,8 +313,7 @@
         k = (s + o) % 8
         t1.append(send(b.u.at[k], b.t1r.at[s], {"section": k}))
     spread_end(far)
-    gate_up(0, far_z)
-    far_rows = [reduce_send(b.g1, b.gr, 0, chunk) for chunk in BOTH]
+    far_rows = gate_up(0, far_z)
     near_rows = [reduce_send(b.g1, b.gr, 1, chunk) for chunk in BOTH]
     stores = [pltpu.make_async_copy(b.nt, outs[0], out_sem.at[0])]
     stores[0].start()
@@ -436,10 +438,10 @@
             c.wait_recv()
         e2.append(spread_start(lambda k, buf=dl[n]: buf.at[:, k]))
 
-    def d_hidden(n, z):
+    def d_hidden(n, z, first=0, last=HW):
         low, high = COLUMNS[n]
         four = jnp.concatenate([dl[n][2 * k + z].reshape(128, high - low) for k in range(4)], axis=0)
-        return dot(b.wd[:, low:high], four, NT)
+        return dot(b.wd[first:last, low:high], four, NT)
 
     spread_forward(e2[0])
     spread_end(e2[0])
@@ -449,10 +451,13 @@
     spread_end(e2[1])
     copies = []
     for h, z in ((0, far_z), (1, zh)):
-        m = (b.hacc[h] + d_hidden(1, z)).astype(BF16)
-        for k in range(4):
-            b.h1[h, k] = m[:, 128 * k : 128 * (k + 1)]
-        copies.append([reduce_send(b.h1, b.hr, h, chunk) for chunk in HIDDEN])
+        sent = []
+        for first, last in HIDDEN:
+            m = (b.hacc[h, first:last] + d_hidden(1, z, first, last)).astype(BF16)
+            for k in range(4):
+                b.h1[h, k, first:last] = m[:, 128 * k : 128 * (k + 1)]
+            sent.append(reduce_send(b.h1, b.hr, h, (first, last)))
+        copies.append(sent)
     gather_end(factors)
     stores.append(pltpu.make_async_copy(b.aa, outs[2], out_sem.at[2]))
     stores[-1].start()

time: 124 us -> 125 us (level)
  no operation moved by 1% of the time
where the time goes in v1:
time: 125 us
  Pallas kernels  124 us (99%)
    pallas_call x1, Pallas kernels, on_device(): pl.pallas_call(kernel, out_shape=[jax.ShapeDtypeStruct(*out) for out in O...  119 us
    pallas_call x1, Pallas kernels, on_device(): pl.pallas_call(gradients, out_shape=[jax.ShapeDtypeStruct((HW, SW), F32)]...  4.87 us

profile of v1, /device:TPU:1, one launch (start us, length us, event | category | flops | bytes accessed | tf_op | source)
XLA Modules:
  0.0 124.9 jit_solution(16321937981119378988)
XLA Ops:
  0.6 119.3 %shard_map.112 = (bf16[4,2,8,80,128]{4,3,2,1,0:T(8,128)(2,1)}, f32[400,640]{1,0:T(8,128)}, bf16[4,2,800,128]{3,2,1,0:T(8,128)(2,1)}, bf16[4,2,400,128]{3,2,1,0:T(8,128)(2,1)}) custom-call(bf16[32,4,4096]{2,1,0:T(4,128)(2,1)} %bitcast.13, s32[8,32]{1,0:T(8,128)} %layer_map.1, s32[8,32]{1,0:T(8,128)} %route.1, bf16[4096,640]{1,0:T(8,128)(2,1)} %proj.1, ...), custom_call_target="tpu_custom_call" | custom-call | tf_op jit(solution)/shard_map/pallas_call | solution.py:548
  120.0 4.9 %shard_map.113 = (f32[400,640]{1,0:T(8,128)}, f32[400,640]{1,0:T(8,128)}, f32[400,640]{1,0:T(8,128)}) custom-call(bf16[8,640,128]{2,1,0:T(8,128)(2,1)} %bitcast.11, f32[400,640]{1,0:T(8,128)} %get-tuple-element.11.down, bf16[8,800,128]{2,1,0:T(8,128)(2,1)} %bitcast.10, bf16[8,400,128]{2,1,0:T(8,128)(2,1)} %bitcast.14), custom_call_target="tpu_custom_call" | custom-call | tf_op jit(solution)/shard_map/pallas_call | solution.py:570
